TPU v7x, 256 devices: a whole 4x4x8 slice. The times are simulated.
256 devices in a mesh: snap: 64 (over x, y_lo, z), bin: 4 (over y_hi, core).
Axes of the slice: x: 4, y: 4 (y_hi: 2, y_lo: 2; y = y_hi * 2 + y_lo), z: 8, core: 2. Of those that a mesh axis runs over, the one named last changes fastest.
Arguments:
- data: bfloat16 [256, 1024, 1024], P(None, ('snap', 'bin')), may hold values from -6 to 6
- steering: bfloat16 [256, 1024, 2048], P(('snap', 'bin')), may hold values from -2 to 2
- start: float32 [256, 1024, 64], P(('snap', 'bin')), may hold values from -6 to 6
Outputs:
- projector: float32 [256, 1024, 1024], P(('snap', 'bin'))
- spectrum: float32 [2048], replicated
All inputs are finite; a program needn't handle non-finite values.
Results may differ from a plain program's by a relative error of at most 0.00042.
Values may be sent and summed in bfloat16 or wider, within the bound.
No kernel may reach another device: no remote copies, remote signals or barrier semaphores. Data moves between devices by JAX's collectives and lax.ppermute only.
A program may use at most 64 MiB of HBM per device.

v0:
```python
import jax
import jax.numpy as jnp
from jax import lax
from jax.sharding import Mesh
from jax.sharding import PartitionSpec as P

M = 1024
F = 256
ITERS = 3
SNAP_BIN = ("snap_0", "snap_1", "snap_2", "bin_0", "bin_1")
SNAP = ("snap_0", "snap_1", "snap_2")
BIN = ("bin_0", "bin_1")


def in_blocks(x, dim, peers):
    before, after = (x.shape[:dim], x.shape[dim + 1 :])
    return jnp.moveaxis(x.reshape(*before, peers, -1, *after), dim, 0)


def laid_out(tiles, dim):
    shape = list(tiles.shape[1:])
    shape[dim] *= tiles.shape[0]
    return jnp.moveaxis(tiles, 0, dim).reshape(shape)


def joined_exchange(x, axis, axes, splits, concats):
    sizes = [lax.axis_size(a) for a in axes]
    tiles = in_blocks(x, splits[0], sizes[0])
    tiles = jnp.moveaxis(in_blocks(tiles, splits[1] + 1, sizes[1]), 0, 1)
    inside = tiles.shape[2:]
    tiles = tiles.reshape(-1, *inside)
    tiles = lax.all_to_all(tiles, axis, split_axis=0, concat_axis=0, tiled=True)
    tiles = laid_out(tiles.reshape(*sizes, *inside), concats[0] + 1)
    return laid_out(tiles, concats[1])


def over_axes(x, axes):
    for axis in axes:
        x = lax.psum(x, axis)
    return x


def one_bin(snaps, steer, basis):
    covar = jnp.dot(snaps.T, snaps, preferred_element_type=jnp.float32) / snaps.shape[0]
    for step in range(ITERS):
        image = jnp.dot(covar, basis, precision=lax.Precision.HIGHEST)
        gram_mat = jnp.dot(image.T, image, precision=lax.Precision.HIGHEST)
        lower_factor = jnp.linalg.cholesky(gram_mat)
        basis = jax.scipy.linalg.solve_triangular(lower_factor, image.T, lower=True).T
    projector = jnp.dot(basis, basis.T, precision=lax.Precision.HIGHEST)
    basis_low = basis.astype(jnp.bfloat16)
    along = jnp.dot(basis_low.T, steer, preferred_element_type=jnp.float32)
    steer_wide = steer.astype(jnp.float32)
    energy = jnp.sum(steer_wide * steer_wide, axis=0)
    noise = energy - jnp.sum(along * along, axis=0)
    return (projector, noise)


def on_device(data, steering, start):
    owned = joined_exchange(data, SNAP_BIN, (SNAP, BIN), (0, 0), (1, 1))
    projector, noise = lax.map(
        lambda items: one_bin(items[0], items[1], items[2]), (owned, steering, start)
    )
    overall = over_axes(jnp.sum(noise, axis=0), SNAP_BIN)
    spectrum = F * M / overall
    return (projector, spectrum)


def solution(mesh):
    finer = Mesh(
        mesh.devices.reshape(4, 2, 8, 2, 2), ("snap_0", "snap_1", "snap_2", "bin_0", "bin_1")
    )
    placed = (P(None, SNAP_BIN, None), P(SNAP_BIN, None, None), P(SNAP_BIN, None, None))
    return jax.shard_map(
        on_device,
        mesh=finer,
        in_specs=placed,
        out_specs=(P(SNAP_BIN, None, None), P()),
        check_vma=False,
    )
```

profile of v0, /device:TPU:32, one launch (start us, length us, event | category | flops | bytes accessed | tf_op | source)
XLA Modules:
  0.0 175.6 jit_solution(7166409924680504966)
XLA Ops:
  0.6 0.0 copy-start
  0.6 14.4 %all-to-all-start = ((bf16[256,1,4,1024]{3,2,1,0:T(4,128)(2,1)}), bf16[256,1,4,1024]{3,2,1,0:T(4,128)(2,1)S(1)}, u32[]{:S(2)}, u32[]{:S(2)}) async-start(bf16[256,1,4,1024]{3,2,1,0:T(4,128)(2,1)} %bitcast.73), calls=%async_computation | async-start | bytes 4194304 | tf_op jit(solution)/shard_map/all_to_all | solution.py:32
  15.0 3.1 %multiply_reduce_fusion = f32[2048]{0:T(1024)S(1)} fusion(bf16[1,1024,2048]{2,1,0:T(8,128)(2,1)} %param.7), kind=kLoop, calls=%fused_computation | loop fusion | flops 6289408 | bytes 4202496 | tf_op jit(solution)/shard_map/while/body/eval_jaxpr/reduce_sum | solution.py:54
  18.1 49.3 %all-to-all-done = bf16[256,1,4,1024]{3,2,1,0:T(4,128)(2,1)S(1)} async-done(((bf16[256,1,4,1024]{3,2,1,0:T(4,128)(2,1)}), bf16[256,1,4,1024]{3,2,1,0:T(4,128)(2,1)S(1)}, u32[]{:S(2)}, u32[]{:S(2)}) %all-to-all-start) | async-done | bytes 2097184 | tf_op jit(solution)/shard_map/all_to_all | solution.py:32
  67.4 5.1 %fusion.8 = f32[1024,1024,1,1]{1,0,3,2:T(8,128)S(1)} fusion(bf16[64,4,1,4,1024]{4,3,1,0,2:T(4,128)(2,1)S(1)} %bitcast.74), kind=kOutput, calls=%fused_computation.9 | convolution fusion | flops 2147483648 | bytes 6291456 | tf_op jit(solution)/shard_map/while/body/eval_jaxpr/dot_general | solution.py:44
  72.5 0.0 copy-start.1
  72.5 2.0 %copy-done.1 = f32[1024,1024,1,1]{1,0,3,2:T(8,128)} copy-done((f32[1024,1024,1,1]{1,0,3,2:T(8,128)}, f32[1024,1024,1,1]{1,0,3,2:T(8,128)S(1)}, u32[]{:S(2)}) %copy-start.1) | copy-done | bytes 4194328
  74.5 0.0 copy-done
  74.5 4.2 %fusion.4 = f32[1024,64]{0,1:T(8,128)S(1)} fusion(f32[1024,1024,1,1]{1,0,3,2:T(8,128)S(1)} %fusion.8, f32[1,1024,64]{1,2,0:T(8,128)S(1)} %copy-done), kind=kOutput, calls=%fused_computation.6 | convolution fusion | flops 806354944 | bytes 4718592 | tf_op jit(solution)/shard_map/while/body/eval_jaxpr/dot_general | solution.py:46
  78.7 0.4 fusion.41
  79.1 0.1 copy.13
  79.2 5.8 %cholesky.59 = f32[64,64]{1,0:T(8,128)S(1)} custom-call(f32[64,64]{1,0:T(8,128)S(1)} %fusion.33), custom_call_target="Cholesky" | custom-call | tf_op jit(solution)/shard_map/while/body/eval_jaxpr/jit(cholesky)/cholesky | solution.py:48
  85.0 0.6 compare_reduce_fusion.2
  85.7 0.7 fusion.25
  86.3 4.9 %custom-call.7 = f32[1,64,64]{1,2,0:T(8,128)S(1)} custom-call(f32[1,64,64]{2,1,0:T(8,128)S(1)} %fusion.25), custom_call_target="InvertDiagBlocksLowerTriangular" | custom-call | tf_op jit(solution)/shard_map/while/body/eval_jaxpr/jit(_solve_triangular)/triangular_solve | solution.py:49
  91.2 0.4 fusion.21
  91.7 6.6 %fusion.3 = f32[1024,64]{0,1:T(8,128)S(1)} fusion(f32[64,1024]{1,0:T(8,128)S(1)} %fusion.21, f32[1024,1024,1,1]{1,0,3,2:T(8,128)} %copy-done.1), kind=kOutput, calls=%fused_computation.5 | convolution fusion | flops 806354944 | bytes 4718592 | tf_op jit(solution)/shard_map/while/body/eval_jaxpr/dot_general | solution.py:46
  98.2 0.4 fusion.42
  98.6 0.1 copy.14
  98.7 5.8 %cholesky.70 = f32[64,64]{1,0:T(8,128)S(1)} custom-call(f32[64,64]{1,0:T(8,128)S(1)} %fusion.31), custom_call_target="Cholesky" | custom-call | tf_op jit(solution)/shard_map/while/body/eval_jaxpr/jit(cholesky)/cholesky | solution.py:48
  104.6 0.6 compare_reduce_fusion.1
  105.2 0.7 fusion.26
  105.9 4.9 %custom-call.8 = f32[1,64,64]{1,2,0:T(8,128)S(1)} custom-call(f32[1,64,64]{2,1,0:T(8,128)S(1)} %fusion.26), custom_call_target="InvertDiagBlocksLowerTriangular" | custom-call | tf_op jit(solution)/shard_map/while/body/eval_jaxpr/jit(_solve_triangular)/triangular_solve | solution.py:49
  110.8 0.4 fusion.19
  111.2 6.4 %fusion.2 = f32[1024,64]{0,1:T(8,128)S(1)} fusion(f32[64,1024]{1,0:T(8,128)S(1)} %fusion.19, f32[1024,1024,1,1]{1,0,3,2:T(8,128)} %copy-done.1), kind=kOutput, calls=%fused_computation.4 | convolution fusion | flops 806354944 | bytes 4718592 | tf_op jit(solution)/shard_map/while/body/eval_jaxpr/dot_general | solution.py:46
  117.6 0.4 fusion.43
  118.0 0.1 copy.15
  118.1 5.8 %cholesky.81 = f32[64,64]{1,0:T(8,128)S(1)} custom-call(f32[64,64]{1,0:T(8,128)S(1)} %fusion.29), custom_call_target="Cholesky" | custom-call | tf_op jit(solution)/shard_map/while/body/eval_jaxpr/jit(cholesky)/cholesky | solution.py:48
  124.0 0.6 compare_reduce_fusion
  124.6 0.7 fusion.27
  125.3 4.9 %custom-call.9 = f32[1,64,64]{1,2,0:T(8,128)S(1)} custom-call(f32[1,64,64]{2,1,0:T(8,128)S(1)} %fusion.27), custom_call_target="InvertDiagBlocksLowerTriangular" | custom-call | tf_op jit(solution)/shard_map/while/body/eval_jaxpr/jit(_solve_triangular)/triangular_solve | solution.py:49
  130.2 0.0 copy-start.2
  130.2 0.4 fusion.17
  130.6 5.0 %convolution_bitcast_fusion = f32[1,1024,1024]{2,1,0:T(8,128)} fusion(f32[64,1024]{1,0:T(8,128)S(1)} %fusion.17), kind=kOutput, calls=%fused_computation.8 | convolution fusion | flops 805306368 | bytes 4456448 | tf_op jit(solution)/shard_map/while/body/eval_jaxpr/dot_general | solution.py:50
  135.6 0.0 copy-done.2
  135.6 0.9 fusion.14
  136.5 9.7 %psum.35 = f32[2048]{0:T(1024)S(1)} all-reduce(f32[2048]{0:T(1024)S(1)} %sub.6), channel_id=1, replica_groups=mesh['snap_0'=4,'snap_1'=2,'snap_2'=8,'bin_0'=2,'bin_1'=2] {'snap_0'}, use_global_device_ids=true, to_apply=%region_4.7 | all-reduce | flops 2048 | bytes 16384 | tf_op jit(solution)/shard_map/psum | solution.py:39
  146.2 5.0 %psum.36 = f32[2048]{0:T(1024)S(1)} all-reduce(f32[2048]{0:T(1024)S(1)} %psum.35), channel_id=1, replica_groups=mesh['snap_0'=4,'snap_1'=2,'snap_2'=8,'bin_0'=2,'bin_1'=2] {'snap_1'}, use_global_device_ids=true, to_apply=%region_5.8 | all-reduce | flops 2048 | bytes 16384 | tf_op jit(solution)/shard_map/psum | solution.py:39
  151.2 14.8 %psum.37 = f32[2048]{0:T(1024)S(1)} all-reduce(f32[2048]{0:T(1024)S(1)} %psum.36), channel_id=1, replica_groups=mesh['snap_0'=4,'snap_1'=2,'snap_2'=8,'bin_0'=2,'bin_1'=2] {'snap_2'}, use_global_device_ids=true, to_apply=%region_6.9 | all-reduce | flops 2048 | bytes 16384 | tf_op jit(solution)/shard_map/psum | solution.py:39
  166.0 6.5 %psum.38 = f32[2048]{0:T(1024)S(1)} all-reduce(f32[2048]{0:T(1024)S(1)} %psum.37), channel_id=1, replica_groups=mesh['snap_0'=4,'snap_1'=2,'snap_2'=8,'bin_0'=2,'bin_1'=2] {'bin_0'}, use_global_device_ids=true, to_apply=%region_7.10 | all-reduce | flops 2048 | bytes 16384 | tf_op jit(solution)/shard_map/psum | solution.py:39
  172.6 2.5 %psum.39 = f32[2048]{0:T(1024)S(1)} all-reduce(f32[2048]{0:T(1024)S(1)} %psum.38), channel_id=1, replica_groups=mesh['snap_0'=4,'snap_1'=2,'snap_2'=8,'bin_0'=2,'bin_1'=2] {'bin_1'}, use_global_device_ids=true, to_apply=%region_8.11 | all-reduce | flops 2048 | bytes 16384 | tf_op jit(solution)/shard_map/psum | solution.py:39
  175.0 0.6 broadcast_divide_fusion
  (7 shorter events, 0.1 us)
Async XLA Ops:
  0.6 73.9 %copy-start = (f32[1,1024,64]{1,2,0:T(8,128)S(1)}, f32[1,1024,64]{1,2,0:T(8,128)}, u32[]{:S(2)}) copy-start(f32[1,1024,64]{1,2,0:T(8,128)} %param.8) | copy-start | bytes 786436
  0.6 66.7 %all-to-all-start = ((bf16[256,1,4,1024]{3,2,1,0:T(4,128)(2,1)}), bf16[256,1,4,1024]{3,2,1,0:T(4,128)(2,1)S(1)}, u32[]{:S(2)}, u32[]{:S(2)}) async-start(bf16[256,1,4,1024]{3,2,1,0:T(4,128)(2,1)} %bitcast.73), calls=%async_computation | async-start | bytes 4194304 | tf_op jit(solution)/shard_map/all_to_all | solution.py:32
  72.5 2.0 %copy-start.1 = (f32[1024,1024,1,1]{1,0,3,2:T(8,128)}, f32[1024,1024,1,1]{1,0,3,2:T(8,128)S(1)}, u32[]{:S(2)}) copy-start(f32[1024,1024,1,1]{1,0,3,2:T(8,128)S(1)} %fusion.8) | copy-start | bytes 12582916
  130.2 5.5 %copy-start.2 = (bf16[1,1024,2048]{2,1,0:T(8,128)(2,1)S(1)}, bf16[1,1024,2048]{2,1,0:T(8,128)(2,1)}, u32[]{:S(2)}) copy-start(bf16[1,1024,2048]{2,1,0:T(8,128)(2,1)} %param.7) | copy-start | bytes 12582916
where the time goes:
time: 179 us; the launch traced here: 176 us
  waiting for transfers between devices  49.3 us (28%)
  other arithmetic  39.9 us (22%)
  blocking collectives  38.5 us (22%)
  matrix products  30.5 us (17%)
  starting transfers between devices  14.4 us (8%)
  local copies, waits for them, and re-layouts  2.25 us (1%)
    all_to_all x1, waiting for transfers between devices, joined_exchange(): tiles = lax.all_to_all(tiles, axis, split_axis=0, concat_axis=0, tiled=True)  49.3 us
    psum x5, blocking collectives, over_axes(): x = lax.psum(x, axis)  38.5 us
    another operation x9, other arithmetic, one_bin(): lower_factor = jnp.linalg.cholesky(gram_mat)  19.6 us
    dot_general x3, matrix products, one_bin(): image = jnp.dot(covar, basis, precision=lax.Precision.HIGHEST)  17.1 us
    another operation x6, other arithmetic, one_bin(): jax.scipy.linalg.solve_triangular(lower_factor, image.T, lower=True)  16.6 us
    all_to_all x1, starting transfers between devices, joined_exchange(): tiles = lax.all_to_all(tiles, axis, split_axis=0, concat_axis=0, tiled=True)  14.4 us
    dot_general x1, matrix products, one_bin(): jnp.dot(snaps.T, snaps, preferred_element_type=jnp.float32) / snaps.shape[0]  5.12 us
    dot_general x1, matrix products, one_bin(): projector = jnp.dot(basis, basis.T, precision=lax.Precision.HIGHEST)  5.03 us
  transfers between devices with their start and end apart: 1, of which 1 were waited for; matrix products, arithmetic and copies ran while one was open for 2% of the time, Pallas kernels for 0%

commit v1 on v0

v1 whole, which is shorter than its diff:
```python
import functools

import jax
import jax.numpy as jnp
from jax import lax
from jax.experimental import pallas as pl
from jax.experimental.pallas import tpu as pltpu
from jax.sharding import Mesh
from jax.sharding import PartitionSpec as P

M = 1024
F = 256
G = 2048
N = 64
ITERS = 3
PARTS = 3
AXES = ("x", "yl", "z2", "z1", "z0", "yh", "c")
PLANE = ("x", "yl", "yh", "c")
PLANE_SIZE = 32
NT = (((1,), (1,)), ((), ()))
NN = (((1,), (0,)), ((), ()))


def dot(a, b, dims):
    return lax.dot_general(a, b, dims, preferred_element_type=jnp.float32)


def split(x, parts):
    out = []
    for _ in range(parts - 1):
        p = x.astype(jnp.bfloat16)
        out.append(p)
        x = x - p.astype(jnp.float32)
    return out + [x.astype(jnp.bfloat16)]


def fold(y, parts):
    s = y[0:N]
    for i in range(1, parts):
        s = s + y[i * N : (i + 1) * N]
    return s


def inverse_factor(gram, beside=None):
    row = lax.broadcasted_iota(jnp.int32, (8, 128), 0)
    lane = lax.broadcasted_iota(jnp.int32, (8, 128), 1)
    a = []
    for q in range(8):
        eye = jnp.where(lane - N == row + 8 * q, 1.0, 0.0).astype(jnp.float32)
        wide = jnp.concatenate([gram[8 * q : 8 * q + 8], jnp.zeros((8, N), jnp.float32)], axis=1)
        a.append(wide + eye)
    done = []
    for j in range(N):
        q0, s = divmod(j, 8)
        pivot_row = a[q0][s : s + 1, :]
        r = lax.rsqrt(jnp.broadcast_to(pivot_row[:, j : j + 1], (1, 128)))
        scaled = pivot_row * r
        done.append(scaled)
        for q in range(q0, 8):
            if q == q0 and s == 7:
                continue
            new = a[q] - (a[q][:, j : j + 1] * r) * scaled
            a[q] = jnp.where(row > s, new, a[q]) if q == q0 else new
        if beside is not None:
            beside(j)
    return jnp.concatenate(done, axis=0)[:, N:]


def subspace_kernel(d_ref, steer_ref, start_ref, noise_ref, left_ref, right_ref, energy_ref):
    def add_energy(j):
        rows = steer_ref[j * (M // N) : (j + 1) * (M // N), :].astype(jnp.float32)
        squares = rows * rows
        part = squares[0:8] + squares[8:16]
        energy_ref[...] = part if j == 0 else energy_ref[...] + part

    basis = start_ref[...]
    for step in range(ITERS):
        y = fold(dot(jnp.concatenate(split(basis, PARTS), 0), d_ref[...], NT), PARTS)
        x = fold(dot(jnp.concatenate(split(y, PARTS), 0), d_ref[...], NN), PARTS) * (1.0 / M)
        xs = jnp.concatenate(split(x, PARTS), 0)
        wide = fold(dot(xs, xs, NT), PARTS)
        gram = wide[:, 0:N]
        for i in range(1, PARTS):
            gram = gram + wide[:, N * i : N * (i + 1)]
        basis = lax.dot_general(
            inverse_factor(gram, add_energy if step == 0 else None),
            x,
            NN,
            precision=lax.Precision.HIGHEST,
            preferred_element_type=jnp.float32,
        )
    hi, lo = split(basis, 2)
    left_ref[...] = jnp.concatenate([hi, hi, lo, lo], 0)
    right_ref[...] = jnp.concatenate([hi, lo, hi, lo], 0)
    along = dot(hi, steer_ref[...], NN)
    energy = jnp.sum(energy_ref[...], axis=0, keepdims=True)
    noise = energy - jnp.sum(along * along, axis=0, keepdims=True)
    for c in range(G // 128):
        piece = noise[:, c * 128 : (c + 1) * 128]
        noise_ref[:, c, :] = jnp.broadcast_to(piece, (PLANE_SIZE, 128))


def subspace(d, steer, start):
    whole = pl.BlockSpec(memory_space=pltpu.VMEM)
    return pl.pallas_call(
        subspace_kernel,
        out_shape=(
            jax.ShapeDtypeStruct((PLANE_SIZE, G // 128, 128), jnp.float32),
            jax.ShapeDtypeStruct((4 * N, M), jnp.bfloat16),
            jax.ShapeDtypeStruct((4 * N, M), jnp.bfloat16),
        ),
        in_specs=[whole] * 3,
        out_specs=(whole, whole, whole),
        scratch_shapes=[pltpu.VMEM((8, G), jnp.float32)],
        compiler_params=pltpu.CompilerParams(vmem_limit_bytes=40 * 2**20),
        name="subspace",
    )(d, steer, start)


def on_device(data, steering, start):
    owned = lax.all_to_all(data, AXES, split_axis=0, concat_axis=0, tiled=True)
    owned = owned.reshape(M, M)
    noise, left, right = subspace(owned, steering[0], start[0].T)
    total = lax.all_to_all(noise, PLANE, split_axis=0, concat_axis=0, tiled=True).sum(0)
    for axis in ("z0", "z1", "z2"):
        total = total + lax.ppermute(total, axis, [(0, 1), (1, 0)])
    projector = lax.dot_general(
        left, right, (((0,), (0,)), ((), ())), preferred_element_type=jnp.float32
    )
    spectrum = F * M / total.reshape(G)
    return (projector[None], spectrum)


def solution(mesh):
    finer = Mesh(mesh.devices.reshape(4, 2, 2, 2, 2, 2, 2), AXES)
    by_bin = P(AXES, None, None)
    return jax.shard_map(
        on_device,
        mesh=finer,
        in_specs=(P(None, AXES, None), by_bin, by_bin),
        out_specs=(by_bin, P()),
        check_vma=False,
    )
```

time: 179 us -> 126 us (0.70); the launches traced: 176 us -> 126 us
  blocking collectives: 38.5 us -> 80.8 us
  other arithmetic: 39.9 us -> 0.65 us
  waiting for transfers between devices: 49.3 us -> 10.5 us
  matrix products: 30.5 us -> 2.76 us
  Pallas kernels: 0 us -> 22.9 us
  starting transfers between devices: 14.4 us -> 2.58 us
  local copies, waits for them, and re-layouts: 2.25 us -> 4.72 us
    all_to_all x0 -> x2, blocking collectives: none -> 80.8 us  [the longest x1 66.8 us: on_device(): owned = lax.all_to_all(data, AXES, split_axis=0, concat_axis=0, tiled=True)]
    all_to_all x1 -> x0, waiting for transfers between devices: 49.3 us -> none  [joined_exchange(): tiles = lax.all_to_all(tiles, axis, split_axis=0, concat_axis=0, tiled=True)]
    psum x5 -> x0, blocking collectives: 38.5 us -> none  [over_axes(): x = lax.psum(x, axis)]
    another operation x15 -> x0, other arithmetic: 36.2 us -> none  [the longest x9 19.6 us: one_bin(): lower_factor = jnp.linalg.cholesky(gram_mat)]
    dot_general x9 -> x1, matrix products: 29.2 us -> 2.76 us  [on_device(): lax.dot_general(left, right, (((0,), (0,)), ((), ())), preferred_element_...]
    pallas_call x0 -> x1, Pallas kernels: none -> 22.9 us  [subspace(): pl.pallas_call(subspace_kernel, out_shape=(jax.ShapeDtypeStruct((PLANE_SI...]
    all_to_all x1 -> x0, starting transfers between devices: 14.4 us -> none  [joined_exchange(): tiles = lax.all_to_all(tiles, axis, split_axis=0, concat_axis=0, tiled=True)]
    ppermute x0 -> x3, waiting for transfers between devices: none -> 10.5 us  [on_device(): total = total + lax.ppermute(total, axis, [(0, 1), (1, 0)])]
  transfers between devices with their start and end apart: 1 -> 3, of which waited for: 1 -> 3; matrix products, arithmetic and copies ran while one was open for 2% -> 2% of each run, Pallas kernels for 0% -> 0%
where the time goes in v1:
time: 126 us
  blocking collectives  80.8 us (64%)
  Pallas kernels  22.9 us (18%)
  waiting for transfers between devices  10.5 us (8%)
  local copies, waits for them, and re-layouts  4.72 us (4%)
  matrix products  2.76 us (2%)
  starting transfers between devices  2.58 us (2%)
    all_to_all x1, blocking collectives, on_device(): owned = lax.all_to_all(data, AXES, split_axis=0, concat_axis=0, tiled=True)  66.8 us
    pallas_call x1, Pallas kernels, subspace(): pl.pallas_call(subspace_kernel, out_shape=(jax.ShapeDtypeStruct((PLANE_SI...  22.9 us
    all_to_all x1, blocking collectives, on_device(): lax.all_to_all(noise, PLANE, split_axis=0, concat_axis=0, tiled=True).sum(0)  14 us
    ppermute x3, waiting for transfers between devices, on_device(): total = total + lax.ppermute(total, axis, [(0, 1), (1, 0)])  10.5 us
    dot_general x1, matrix products, on_device(): lax.dot_general(left, right, (((0,), (0,)), ((), ())), preferred_element_...  2.76 us
    ppermute x3, starting transfers between devices, on_device(): total = total + lax.ppermute(total, axis, [(0, 1), (1, 0)])  2.58 us
    reshape x1, local copies, waits for them, and re-layouts, on_device(): owned = owned.reshape(M, M)  2.54 us
  transfers between devices with their start and end apart: 3, of which 3 were waited for; matrix products, arithmetic and copies ran while one was open for 2% of the time, Pallas kernels for 0%

profile of v1, /device:TPU:32, one launch (start us, length us, event | category | flops | bytes accessed | tf_op | source)
XLA Modules:
  0.0 125.6 jit_solution(3835843241172436165)
XLA Ops:
  0.6 0.0 copy-start.1
  0.6 66.8 %all_to_all.10 = bf16[256,4,1024]{2,1,0:T(4,128)(2,1)} all-to-all(bf16[256,4,1024]{2,1,0:T(4,128)(2,1)} %param.3), channel_id=1, replica_groups=mesh['x'=4,'yl'=2,'z2'=2,'z1'=2,'z0'=2,'yh'=2,'c'=2] {'x','yl','z2','z1'..., dimensions={0} | all-to-all | bytes 4194304 | tf_op jit(solution)/shard_map/all_to_all | solution.py:121
  67.5 2.5 %reshape.10.d_ref = bf16[1024,1024]{1,0:T(8,128)(2,1)S(1)} reshape(bf16[256,4,1024]{2,1,0:T(4,128)(2,1)} %all_to_all.10) | data formatting | bytes 4194304 | tf_op jit(solution)/shard_map/reshape | solution.py:122
  70.0 0.0 copy-done.1
  70.0 0.0 copy-start
  70.0 2.2 %copy-done = bf16[1,1024,2048]{2,1,0:T(8,128)(2,1)S(1)} copy-done((bf16[1,1024,2048]{2,1,0:T(8,128)(2,1)S(1)}, bf16[1,1024,2048]{2,1,0:T(8,128)(2,1)}, u32[]{:S(2)}) %copy-start) | copy-done | bytes 4194328
  72.2 22.9 %subspace.1 = (f32[32,16,128]{2,1,0:T(8,128)S(1)}, bf16[256,1024]{1,0:T(8,128)(2,1)S(1)}, bf16[256,1024]{1,0:T(8,128)(2,1)S(1)}) custom-call(bf16[1024,1024]{1,0:T(8,128)(2,1)S(1)} %reshape.10.d_ref, bf16[1024,2048]{1,0:T(8,128)(2,1)S(1)} %bitcast.10, f32[64,1024]{1,0:T(8,128)S(1)} %bitcast.11), custom_call_target="tpu_custom_call" | custom-call | tf_op jit(solution)/shard_map/subspace/pallas_call | solution.py:105
  95.2 14.0 %all_to_all.11 = f32[32,16,128]{2,1,0:T(8,128)S(1)} all-to-all(f32[32,16,128]{2,1,0:T(8,128)S(1)} %get-tuple-element.7), channel_id=1, replica_groups=mesh['x'=4,'yl'=2,'z2'=2,'z1'=2,'z0'=2,'yh'=2,'c'=2] {'x','yl','yh','c'}, dimensions={0} | all-to-all | bytes 524288 | tf_op jit(solution)/shard_map/all_to_all | solution.py:124
  109.2 1.1 collective-permute-start
  110.3 2.6 %collective-permute-done = f32[16,128]{1,0:T(8,128)S(1)} collective-permute-done((f32[16,128]{1,0:T(8,128)S(1)}, f32[16,128]{1,0:T(8,128)S(1)}, u32[]{:S(2)}, u32[]{:S(2)}) %collective-permute-start) | collective-permute-done | bytes 8224 | tf_op jit(solution)/shard_map/ppermute | solution.py:126
  112.9 0.4 collective-permute-start.1
  113.3 4.1 %collective-permute-done.1 = f32[16,128]{1,0:T(8,128)S(1)} collective-permute-done((f32[16,128]{1,0:T(8,128)S(1)}, f32[16,128]{1,0:T(8,128)S(1)}, u32[]{:S(2)}, u32[]{:S(2)}) %collective-permute-start.1) | collective-permute-done | bytes 8224 | tf_op jit(solution)/shard_map/ppermute | solution.py:126
  117.5 1.1 collective-permute-start.2
  118.5 2.8 %convolution_bitcast_fusion = f32[1,1024,1024]{2,1,0:T(8,128)} fusion(bf16[256,1024]{1,0:T(8,128)(2,1)S(1)} %get-tuple-element.5, bf16[256,1024]{1,0:T(8,128)(2,1)S(1)} %get-tuple-element.6), kind=kOutput, calls=%fused_computation | convolution fusion | flops 536870912 | bytes 5242880 | tf_op jit(solution)/shard_map/dot_general | solution.py:127
  121.3 3.7 %collective-permute-done.2 = f32[16,128]{1,0:T(8,128)S(1)} collective-permute-done((f32[16,128]{1,0:T(8,128)S(1)}, f32[16,128]{1,0:T(8,128)S(1)}, u32[]{:S(2)}, u32[]{:S(2)}) %collective-permute-start.2) | collective-permute-done | bytes 8224 | tf_op jit(solution)/shard_map/ppermute | solution.py:126
  125.0 0.6 divide_bitcast_fusion
  (3 shorter events, 0.0 us)
Async XLA Ops:
  0.6 69.4 %copy-start.1 = (f32[1,1024,64]{1,2,0:T(8,128)S(1)}, f32[1,1024,64]{1,2,0:T(8,128)}, u32[]{:S(2)}) copy-start(f32[1,1024,64]{1,2,0:T(8,128)} %param.5) | copy-start | bytes 786436
  70.0 2.2 %copy-start = (bf16[1,1024,2048]{2,1,0:T(8,128)(2,1)S(1)}, bf16[1,1024,2048]{2,1,0:T(8,128)(2,1)}, u32[]{:S(2)}) copy-start(bf16[1,1024,2048]{2,1,0:T(8,128)(2,1)} %param.4) | copy-start | bytes 12582916
  109.2 3.7 %collective-permute-start = (f32[16,128]{1,0:T(8,128)S(1)}, f32[16,128]{1,0:T(8,128)S(1)}, u32[]{:S(2)}, u32[]{:S(2)}) collective-permute-start(f32[16,128]{1,0:T(8,128)S(1)} %reduce_sum.9), channel_id=1, source_target_pairs={{0,4},{4,0},{1,5},{5,1},{2,6},{6,2},{3,7},{7,3},{8,12},{12,8},{9,1... | collective-permute-start | bytes 24584 | tf_op jit(solution)/shard_map/ppermute | solution.py:126
  112.9 4.5 %collective-permute-start.1 = (f32[16,128]{1,0:T(8,128)S(1)}, f32[16,128]{1,0:T(8,128)S(1)}, u32[]{:S(2)}, u32[]{:S(2)}) collective-permute-start(f32[16,128]{1,0:T(8,128)S(1)} %add.9), channel_id=1, source_target_pairs={{0,8},{8,0},{1,9},{9,1},{2,10},{10,2},{3,11},{11,3},{4,12},{12,4},... | collective-permute-start | bytes 24584 | tf_op jit(solution)/shard_map/ppermute | solution.py:126
  117.5 7.6 %collective-permute-start.2 = (f32[16,128]{1,0:T(8,128)S(1)}, f32[16,128]{1,0:T(8,128)S(1)}, u32[]{:S(2)}, u32[]{:S(2)}) collective-permute-start(f32[16,128]{1,0:T(8,128)S(1)} %add.10), channel_id=1, source_target_pairs={{0,16},{16,0},{1,17},{17,1},{2,18},{18,2},{3,19},{19,3},{4,20},{20... | collective-permute-start | bytes 24584 | tf_op jit(solution)/shard_map/ppermute | solution.py:126

commit v2 on v1

--- a/solution.py
+++ b/solution.py
@@ -41,55 +41,115 @@
     return s
 
 
-def inverse_factor(gram, beside=None):
+def stacked(x):
+    return jnp.concatenate(split(x, PARTS), 0)
+
+
+def product(a, b):
+    ah, am, al = split(a, 3)
+    bh, bm, bl = split(b, 3)
+    left = jnp.concatenate([ah, ah, am, am, ah, al], 1)
+    right = jnp.concatenate([bh, bm, bh, bm, bl, bh], 0)
+    return dot(left, right, NN)
+
+
+def gram_of(xs):
+    wide = fold(dot(xs, xs, NT), PARTS)
+    gram = wide[:, 0:N]
+    for i in range(1, PARTS):
+        gram = gram + wide[:, N * i : N * (i + 1)]
+    return gram
+
+
+def lanes(x, j):
+    return jnp.broadcast_to(x[:, j : j + 1], (8, 128))
+
+
+def rows(x, s):
+    return jnp.broadcast_to(x[s : s + 1, :], (8, 128))
+
+
+def inverse_factor(gram, beside):
     row = lax.broadcasted_iota(jnp.int32, (8, 128), 0)
     lane = lax.broadcasted_iota(jnp.int32, (8, 128), 1)
+    blocks = N // 8
     a = []
-    for q in range(8):
+    for q in range(blocks):
         eye = jnp.where(lane - N == row + 8 * q, 1.0, 0.0).astype(jnp.float32)
         wide = jnp.concatenate([gram[8 * q : 8 * q + 8], jnp.zeros((8, N), jnp.float32)], axis=1)
         a.append(wide + eye)
     done = []
-    for j in range(N):
-        q0, s = divmod(j, 8)
-        pivot_row = a[q0][s : s + 1, :]
-        r = lax.rsqrt(jnp.broadcast_to(pivot_row[:, j : j + 1], (1, 128)))
-        scaled = pivot_row * r
-        done.append(scaled)
-        for q in range(q0, 8):
-            if q == q0 and s == 7:
-                continue
-            new = a[q] - (a[q][:, j : j + 1] * r) * scaled
-            a[q] = jnp.where(row > s, new, a[q]) if q == q0 else new
-        if beside is not None:
-            beside(j)
+    for k in range(blocks):
+        below = range(k, blocks)
+        cols = [[lanes(a[q], 8 * k + i) for q in below] for i in range(8)]
+        scaled = []
+        for i in range(8):
+            r = lax.rsqrt(rows(cols[i][0], i))
+            l = [c * r for c in cols[i]]
+            cols[i] = l
+            for i2 in range(i + 1, 8):
+                t = rows(l[0], i2)
+                cols[i2] = [c - m * t for c, m in zip(cols[i2], l)]
+            this = rows(a[k], i)
+            for i1 in range(i):
+                this = this - rows(cols[i1][0], i) * scaled[i1]
+            scaled.append(this * r)
+        out = scaled[0]
+        for i in range(1, 8):
+            out = jnp.where(row == i, scaled[i], out)
+        done.append(out)
+        for q in range(k + 1, blocks):
+            for i in range(8):
+                a[q] = a[q] - cols[i][q - k] * scaled[i]
+        beside(k)
     return jnp.concatenate(done, axis=0)[:, N:]
 
 
-def subspace_kernel(d_ref, steer_ref, start_ref, noise_ref, left_ref, right_ref, energy_ref):
+def subspace_kernel(d_ref, steer_hbm, start_ref, noise_ref, left_ref, right_ref, steer_ref, y_ref, w_ref, energy_ref, sem):
+    fetch = pltpu.make_async_copy(steer_hbm, steer_ref, sem)
+    fetch.start()
+
+    def back(s, j):
+        cut = pl.ds(j * (M // 4), M // 4)
+        y_ref[:, cut] = fold(dot(s, d_ref[cut, :], NT), PARTS)
+
+    def forth(s, j):
+        cut = pl.ds(j * (M // 4), M // 4)
+        w_ref[:, cut] = fold(dot(s, d_ref[:, cut], NN), PARTS) * (1.0 / M)
+
     def add_energy(j):
-        rows = steer_ref[j * (M // N) : (j + 1) * (M // N), :].astype(jnp.float32)
-        squares = rows * rows
-        part = squares[0:8] + squares[8:16]
+        block = steer_ref[j * (M // 8) : (j + 1) * (M // 8), :].astype(jnp.float32)
+        squares = block * block
+        part = jnp.sum(squares.reshape(M // 64, 8, G), axis=0)
         energy_ref[...] = part if j == 0 else energy_ref[...] + part
 
-    basis = start_ref[...]
+    ss = stacked(start_ref[...])
+    for j in range(4):
+        back(ss, j)
+    ss = stacked(y_ref[...])
+    for j in range(4):
+        forth(ss, j)
+    x = w_ref[...]
     for step in range(ITERS):
-        y = fold(dot(jnp.concatenate(split(basis, PARTS), 0), d_ref[...], NT), PARTS)
-        x = fold(dot(jnp.concatenate(split(y, PARTS), 0), d_ref[...], NN), PARTS) * (1.0 / M)
-        xs = jnp.concatenate(split(x, PARTS), 0)
-        wide = fold(dot(xs, xs, NT), PARTS)
-        gram = wide[:, 0:N]
-        for i in range(1, PARTS):
-            gram = gram + wide[:, N * i : N * (i + 1)]
-        basis = lax.dot_general(
-            inverse_factor(gram, add_energy if step == 0 else None),
-            x,
-            NN,
-            precision=lax.Precision.HIGHEST,
-            preferred_element_type=jnp.float32,
-        )
-    hi, lo = split(basis, 2)
+        xs = stacked(x)
+        last = step == ITERS - 1
+        held = [None]
+
+        def beside(k):
+            if last:
+                add_energy(k)
+            elif k < 4:
+                back(xs, k)
+            else:
+                if k == 4:
+                    held[0] = stacked(y_ref[...])
+                forth(held[0], k - 4)
+
+        if last:
+            fetch.wait()
+        inverse = inverse_factor(gram_of(xs), beside)
+        x = product(inverse, x if last else w_ref[...])
+    hi, lo = split(x, 2)
     left_ref[...] = jnp.concatenate([hi, hi, lo, lo], 0)
     right_ref[...] = jnp.concatenate([hi, lo, hi, lo], 0)
     along = dot(hi, steer_ref[...], NN)
@@ -109,9 +169,15 @@
             jax.ShapeDtypeStruct((4 * N, M), jnp.bfloat16),
             jax.ShapeDtypeStruct((4 * N, M), jnp.bfloat16),
         ),
-        in_specs=[whole] * 3,
+        in_specs=[whole, pl.BlockSpec(memory_space=pltpu.HBM), whole],
         out_specs=(whole, whole, whole),
-        scratch_shapes=[pltpu.VMEM((8, G), jnp.float32)],
+        scratch_shapes=[
+            pltpu.VMEM((M, G), jnp.bfloat16),
+            pltpu.VMEM((N, M), jnp.float32),
+            pltpu.VMEM((N, M), jnp.float32),
+            pltpu.VMEM((8, G), jnp.float32),
+            pltpu.SemaphoreType.DMA,
+        ],
         compiler_params=pltpu.CompilerParams(vmem_limit_bytes=40 * 2**20),
         name="subspace",
     )(d, steer, start)

time: 126 us -> 113 us (0.90)
  Pallas kernels: 22.9 us -> 9.85 us
    pallas_call x1, Pallas kernels: 22.9 us -> 9.85 us  [subspace(): pl.pallas_call(subspace_kernel, out_shape=(jax.ShapeDtypeStruct((PLANE_SI...]
where the time goes in v2:
time: 113 us
  blocking collectives  80.8 us (72%)
  waiting for transfers between devices  10.5 us (9%)
  Pallas kernels  9.85 us (9%)
  local copies, waits for them, and re-layouts  4.72 us (4%)
  matrix products  2.76 us (2%)
  starting transfers between devices  2.58 us (2%)
    all_to_all x1, blocking collectives, on_device(): owned = lax.all_to_all(data, AXES, split_axis=0, concat_axis=0, tiled=True)  66.8 us
    all_to_all x1, blocking collectives, on_device(): lax.all_to_all(noise, PLANE, split_axis=0, concat_axis=0, tiled=True).sum(0)  13.9 us
    ppermute x3, waiting for transfers between devices, on_device(): total = total + lax.ppermute(total, axis, [(0, 1), (1, 0)])  10.5 us
    pallas_call x1, Pallas kernels, subspace(): pl.pallas_call(subspace_kernel, out_shape=(jax.ShapeDtypeStruct((PLANE_SI...  9.85 us
    dot_general x1, matrix products, on_device(): lax.dot_general(left, right, (((0,), (0,)), ((), ())), preferred_element_...  2.76 us
    ppermute x3, starting transfers between devices, on_device(): total = total + lax.ppermute(total, axis, [(0, 1), (1, 0)])  2.58 us
    reshape x1, local copies, waits for them, and re-layouts, on_device(): owned = owned.reshape(M, M)  2.54 us
  transfers between devices with their start and end apart: 3, of which 3 were waited for; matrix products, arithmetic and copies ran while one was open for 2% of the time, Pallas kernels for 0%

profile of v2, /device:TPU:32, one launch (start us, length us, event | category | flops | bytes accessed | tf_op | source)
XLA Modules:
  0.0 112.5 jit_solution(9440333356674261401)
XLA Ops:
  0.6 0.0 copy-start.1
  0.6 66.8 %all_to_all.10 = bf16[256,4,1024]{2,1,0:T(4,128)(2,1)} all-to-all(bf16[256,4,1024]{2,1,0:T(4,128)(2,1)} %param.3), channel_id=1, replica_groups=mesh['x'=4,'yl'=2,'z2'=2,'z1'=2,'z0'=2,'yh'=2,'c'=2] {'x','yl','z2','z1'..., dimensions={0} | all-to-all | bytes 4194304 | tf_op jit(solution)/shard_map/all_to_all | solution.py:187
  67.5 2.5 %reshape.10.d_ref = bf16[1024,1024]{1,0:T(8,128)(2,1)S(1)} reshape(bf16[256,4,1024]{2,1,0:T(4,128)(2,1)} %all_to_all.10) | data formatting | bytes 4194304 | tf_op jit(solution)/shard_map/reshape | solution.py:188
  70.0 0.0 copy-done.1
  70.0 0.0 copy-start
  70.0 2.2 %copy-done = bf16[1,1024,2048]{2,1,0:T(8,128)(2,1)S(1)} copy-done((bf16[1,1024,2048]{2,1,0:T(8,128)(2,1)S(1)}, bf16[1,1024,2048]{2,1,0:T(8,128)(2,1)}, u32[]{:S(2)}) %copy-start) | copy-done | bytes 4194328
  72.2 9.9 %subspace.1 = (f32[32,16,128]{2,1,0:T(8,128)S(1)}, bf16[256,1024]{1,0:T(8,128)(2,1)S(1)}, bf16[256,1024]{1,0:T(8,128)(2,1)S(1)}) custom-call(bf16[1024,1024]{1,0:T(8,128)(2,1)S(1)} %reshape.10.d_ref, bf16[1024,2048]{1,0:T(8,128)(2,1)S(1)} %bitcast.10, f32[64,1024]{1,0:T(8,128)S(1)} %bitcast.11), custom_call_target="tpu_custom_call" | custom-call | tf_op jit(solution)/shard_map/subspace/pallas_call | solution.py:165
  82.1 13.9 %all_to_all.11 = f32[32,16,128]{2,1,0:T(8,128)S(1)} all-to-all(f32[32,16,128]{2,1,0:T(8,128)S(1)} %get-tuple-element.7), channel_id=1, replica_groups=mesh['x'=4,'yl'=2,'z2'=2,'z1'=2,'z0'=2,'yh'=2,'c'=2] {'x','yl','yh','c'}, dimensions={0} | all-to-all | bytes 524288 | tf_op jit(solution)/shard_map/all_to_all | solution.py:190
  96.1 1.1 collective-permute-start
  97.2 2.6 %collective-permute-done = f32[16,128]{1,0:T(8,128)S(1)} collective-permute-done((f32[16,128]{1,0:T(8,128)S(1)}, f32[16,128]{1,0:T(8,128)S(1)}, u32[]{:S(2)}, u32[]{:S(2)}) %collective-permute-start) | collective-permute-done | bytes 8224 | tf_op jit(solution)/shard_map/ppermute | solution.py:192
  99.8 0.4 collective-permute-start.1
  100.2 4.1 %collective-permute-done.1 = f32[16,128]{1,0:T(8,128)S(1)} collective-permute-done((f32[16,128]{1,0:T(8,128)S(1)}, f32[16,128]{1,0:T(8,128)S(1)}, u32[]{:S(2)}, u32[]{:S(2)}) %collective-permute-start.1) | collective-permute-done | bytes 8224 | tf_op jit(solution)/shard_map/ppermute | solution.py:192
  104.4 1.1 collective-permute-start.2
  105.4 2.8 %convolution_bitcast_fusion = f32[1,1024,1024]{2,1,0:T(8,128)} fusion(bf16[256,1024]{1,0:T(8,128)(2,1)S(1)} %get-tuple-element.5, bf16[256,1024]{1,0:T(8,128)(2,1)S(1)} %get-tuple-element.6), kind=kOutput, calls=%fused_computation | convolution fusion | flops 536870912 | bytes 5242880 | tf_op jit(solution)/shard_map/dot_general | solution.py:193
  108.2 3.7 %collective-permute-done.2 = f32[16,128]{1,0:T(8,128)S(1)} collective-permute-done((f32[16,128]{1,0:T(8,128)S(1)}, f32[16,128]{1,0:T(8,128)S(1)}, u32[]{:S(2)}, u32[]{:S(2)}) %collective-permute-start.2) | collective-permute-done | bytes 8224 | tf_op jit(solution)/shard_map/ppermute | solution.py:192
  111.9 0.6 divide_bitcast_fusion
  (3 shorter events, 0.0 us)
Async XLA Ops:
  0.6 69.4 %copy-start.1 = (f32[1,1024,64]{1,2,0:T(8,128)S(1)}, f32[1,1024,64]{1,2,0:T(8,128)}, u32[]{:S(2)}) copy-start(f32[1,1024,64]{1,2,0:T(8,128)} %param.5) | copy-start | bytes 786436
  70.0 2.2 %copy-start = (bf16[1,1024,2048]{2,1,0:T(8,128)(2,1)S(1)}, bf16[1,1024,2048]{2,1,0:T(8,128)(2,1)}, u32[]{:S(2)}) copy-start(bf16[1,1024,2048]{2,1,0:T(8,128)(2,1)} %param.4) | copy-start | bytes 12582916
  96.1 3.7 %collective-permute-start = (f32[16,128]{1,0:T(8,128)S(1)}, f32[16,128]{1,0:T(8,128)S(1)}, u32[]{:S(2)}, u32[]{:S(2)}) collective-permute-start(f32[16,128]{1,0:T(8,128)S(1)} %reduce_sum.9), channel_id=1, source_target_pairs={{0,4},{4,0},{1,5},{5,1},{2,6},{6,2},{3,7},{7,3},{8,12},{12,8},{9,1... | collective-permute-start | bytes 24584 | tf_op jit(solution)/shard_map/ppermute | solution.py:192
  99.8 4.5 %collective-permute-start.1 = (f32[16,128]{1,0:T(8,128)S(1)}, f32[16,128]{1,0:T(8,128)S(1)}, u32[]{:S(2)}, u32[]{:S(2)}) collective-permute-start(f32[16,128]{1,0:T(8,128)S(1)} %add.9), channel_id=1, source_target_pairs={{0,8},{8,0},{1,9},{9,1},{2,10},{10,2},{3,11},{11,3},{4,12},{12,4},... | collective-permute-start | bytes 24584 | tf_op jit(solution)/shard_map/ppermute | solution.py:192
  104.4 7.6 %collective-permute-start.2 = (f32[16,128]{1,0:T(8,128)S(1)}, f32[16,128]{1,0:T(8,128)S(1)}, u32[]{:S(2)}, u32[]{:S(2)}) collective-permute-start(f32[16,128]{1,0:T(8,128)S(1)} %add.10), channel_id=1, source_target_pairs={{0,16},{16,0},{1,17},{17,1},{2,18},{18,2},{3,19},{19,3},{4,20},{20... | collective-permute-start | bytes 24584 | tf_op jit(solution)/shard_map/ppermute | solution.py:192

commit v3 on v2

--- a/solution.py
+++ b/solution.py
@@ -14,6 +14,7 @@
 N = 64
 ITERS = 3
 PARTS = 3
+CHUNKS = 4
 AXES = ("x", "yl", "z2", "z1", "z0", "yh", "c")
 PLANE = ("x", "yl", "yh", "c")
 PLANE_SIZE = 32
@@ -105,7 +106,10 @@
     return jnp.concatenate(done, axis=0)[:, N:]
 
 
-def subspace_kernel(d_ref, steer_hbm, start_ref, noise_ref, left_ref, right_ref, steer_ref, y_ref, w_ref, energy_ref, sem):
+def subspace_kernel(
+    data_ref, steer_hbm, start_ref, noise_ref, left_ref, right_ref, d_ref, steer_ref, y_ref, w_ref, energy_ref, sem
+):
+    per = F // CHUNKS
     fetch = pltpu.make_async_copy(steer_hbm, steer_ref, sem)
     fetch.start()
 
@@ -124,7 +128,8 @@
         energy_ref[...] = part if j == 0 else energy_ref[...] + part
 
     ss = stacked(start_ref[...])
-    for j in range(4):
+    for j in range(CHUNKS):
+        d_ref[j * per * 4 : (j + 1) * per * 4, :] = data_ref[j * per : (j + 1) * per].reshape(per * 4, M)
         back(ss, j)
     ss = stacked(y_ref[...])
     for j in range(4):
@@ -160,8 +165,9 @@
         noise_ref[:, c, :] = jnp.broadcast_to(piece, (PLANE_SIZE, 128))
 
 
-def subspace(d, steer, start):
+def subspace(data, steer, start):
     whole = pl.BlockSpec(memory_space=pltpu.VMEM)
+    far = pl.BlockSpec(memory_space=pltpu.HBM)
     return pl.pallas_call(
         subspace_kernel,
         out_shape=(
@@ -169,27 +175,28 @@
             jax.ShapeDtypeStruct((4 * N, M), jnp.bfloat16),
             jax.ShapeDtypeStruct((4 * N, M), jnp.bfloat16),
         ),
-        in_specs=[whole, pl.BlockSpec(memory_space=pltpu.HBM), whole],
+        in_specs=[whole, far, whole],
         out_specs=(whole, whole, whole),
         scratch_shapes=[
+            pltpu.VMEM((M, M), jnp.bfloat16),
             pltpu.VMEM((M, G), jnp.bfloat16),
             pltpu.VMEM((N, M), jnp.float32),
             pltpu.VMEM((N, M), jnp.float32),
             pltpu.VMEM((8, G), jnp.float32),
             pltpu.SemaphoreType.DMA,
         ],
-        compiler_params=pltpu.CompilerParams(vmem_limit_bytes=40 * 2**20),
+        compiler_params=pltpu.CompilerParams(vmem_limit_bytes=52_000_000),
         name="subspace",
-    )(d, steer, start)
+    )(data, steer, start)
 
 
 def on_device(data, steering, start):
     owned = lax.all_to_all(data, AXES, split_axis=0, concat_axis=0, tiled=True)
-    owned = owned.reshape(M, M)
     noise, left, right = subspace(owned, steering[0], start[0].T)
     total = lax.all_to_all(noise, PLANE, split_axis=0, concat_axis=0, tiled=True).sum(0)
-    for axis in ("z0", "z1", "z2"):
+    for axis in ("z0", "z1"):
         total = total + lax.ppermute(total, axis, [(0, 1), (1, 0)])
+    total = total + lax.ppermute(total, ("z2", "z1", "z0"), [(z, 7 - z) for z in range(8)])
     projector = lax.dot_general(
         left, right, (((0,), (0,)), ((), ())), preferred_element_type=jnp.float32
     )

time: 113 us -> 107 us (0.947)
  local copies, waits for them, and re-layouts: 4.72 us -> 0.01 us
  waiting for transfers between devices: 10.5 us -> 9.2 us
    ppermute x3 -> x2, waiting for transfers between devices: 10.5 us -> 6.76 us  [on_device(): total = total + lax.ppermute(total, axis, [(0, 1), (1, 0)])]
    reshape x1 -> x0, local copies, waits for them, and re-layouts: 2.54 us -> none  [on_device(): owned = owned.reshape(M, M)]
    ppermute x0 -> x1, waiting for transfers between devices: none -> 2.43 us  [on_device(): lax.ppermute(total, ('z2', 'z1', 'z0'), [(z, 7 - z) for z in range(8)])]
    unnamed x4 -> x2, local copies, waits for them, and re-layouts: 2.19 us -> 0.01 us
    ppermute x0 -> x1, starting transfers between devices: none -> 1.46 us  [on_device(): lax.ppermute(total, ('z2', 'z1', 'z0'), [(z, 7 - z) for z in range(8)])]
    ppermute x3 -> x2, starting transfers between devices: 2.58 us -> 1.52 us  [on_device(): total = total + lax.ppermute(total, axis, [(0, 1), (1, 0)])]
  transfers between devices with their start and end apart: 3 -> 3, of which waited for: 3 -> 3; matrix products, arithmetic and copies ran while one was open for 2% -> 3% of each run, Pallas kernels for 0% -> 0%
where the time goes in v3:
time: 107 us
  blocking collectives  80.7 us (75%)
  Pallas kernels  9.59 us (9%)
  waiting for transfers between devices  9.2 us (9%)
  starting transfers between devices  2.99 us (3%)
  matrix products  2.76 us (3%)
    all_to_all x1, blocking collectives, on_device(): owned = lax.all_to_all(data, AXES, split_axis=0, concat_axis=0, tiled=True)  66.7 us
    all_to_all x1, blocking collectives, on_device(): lax.all_to_all(noise, PLANE, split_axis=0, concat_axis=0, tiled=True).sum(0)  13.9 us
    pallas_call x1, Pallas kernels, subspace(): pl.pallas_call(subspace_kernel, out_shape=(jax.ShapeDtypeStruct((PLANE_SI...  9.59 us
    ppermute x2, waiting for transfers between devices, on_device(): total = total + lax.ppermute(total, axis, [(0, 1), (1, 0)])  6.76 us
    dot_general x1, matrix products, on_device(): lax.dot_general(left, right, (((0,), (0,)), ((), ())), preferred_element_...  2.76 us
    ppermute x1, waiting for transfers between devices, on_device(): lax.ppermute(total, ('z2', 'z1', 'z0'), [(z, 7 - z) for z in range(8)])  2.43 us
  transfers between devices with their start and end apart: 3, of which 3 were waited for; matrix products, arithmetic and copies ran while one was open for 3% of the time, Pallas kernels for 0%

profile of v3, /device:TPU:32, one launch (start us, length us, event | category | flops | bytes accessed | tf_op | source)
XLA Modules:
  0.0 106.5 jit_solution(2825940521755872719)
XLA Ops:
  0.6 0.0 copy-start
  0.6 66.7 %all_to_all.10.data_ref = bf16[256,4,1024]{2,1,0:T(4,128)(2,1)S(1)} all-to-all(bf16[256,4,1024]{2,1,0:T(4,128)(2,1)} %param.3), channel_id=1, replica_groups=mesh['x'=4,'yl'=2,'z2'=2,'z1'=2,'z0'=2,'yh'=2,'c'=2] {'x','yl','z2','z1'..., dimensions={0} | all-to-all | bytes 4194304 | tf_op jit(solution)/shard_map/all_to_all | solution.py:194
  67.4 0.0 copy-done
  67.4 9.6 %subspace.1 = (f32[32,16,128]{2,1,0:T(8,128)S(1)}, bf16[256,1024]{1,0:T(8,128)(2,1)S(1)}, bf16[256,1024]{1,0:T(8,128)(2,1)S(1)}) custom-call(bf16[256,4,1024]{2,1,0:T(4,128)(2,1)S(1)} %all_to_all.10.data_ref, bf16[1024,2048]{1,0:T(8,128)(2,1)} %bitcast.11, f32[64,1024]{1,0:T(8,128)S(1)} %bitcast.10), custom_call_target="tpu_custom_call" | custom-call | tf_op jit(solution)/shard_map/subspace/pallas_call | solution.py:171
  77.0 13.9 %all_to_all.11 = f32[32,16,128]{2,1,0:T(8,128)S(1)} all-to-all(f32[32,16,128]{2,1,0:T(8,128)S(1)} %get-tuple-element.7), channel_id=1, replica_groups=mesh['x'=4,'yl'=2,'z2'=2,'z1'=2,'z0'=2,'yh'=2,'c'=2] {'x','yl','yh','c'}, dimensions={0} | all-to-all | bytes 524288 | tf_op jit(solution)/shard_map/all_to_all | solution.py:196
  91.0 1.1 %collective-permute-start = (f32[16,128]{1,0:T(8,128)S(1)}, f32[16,128]{1,0:T(8,128)S(1)}, u32[]{:S(2)}, u32[]{:S(2)}) collective-permute-start(f32[16,128]{1,0:T(8,128)S(1)} %reduce_sum.9), channel_id=1, source_target_pairs={{0,4},{4,0},{1,5},{5,1},{2,6},{6,2},{3,7},{7,3},{8,12},{12,8},{9,1... | collective-permute-start | bytes 24584 | tf_op jit(solution)/shard_map/ppermute | solution.py:198
  92.1 2.6 %collective-permute-done = f32[16,128]{1,0:T(8,128)S(1)} collective-permute-done((f32[16,128]{1,0:T(8,128)S(1)}, f32[16,128]{1,0:T(8,128)S(1)}, u32[]{:S(2)}, u32[]{:S(2)}) %collective-permute-start) | collective-permute-done | bytes 8224 | tf_op jit(solution)/shard_map/ppermute | solution.py:198
  94.7 0.4 collective-permute-start.1
  95.1 4.1 %collective-permute-done.1 = f32[16,128]{1,0:T(8,128)S(1)} collective-permute-done((f32[16,128]{1,0:T(8,128)S(1)}, f32[16,128]{1,0:T(8,128)S(1)}, u32[]{:S(2)}, u32[]{:S(2)}) %collective-permute-start.1) | collective-permute-done | bytes 8224 | tf_op jit(solution)/shard_map/ppermute | solution.py:198
  99.2 1.5 %collective-permute-start.2 = (f32[16,128]{1,0:T(8,128)S(1)}, f32[16,128]{1,0:T(8,128)S(1)}, u32[]{:S(2)}, u32[]{:S(2)}) collective-permute-start(f32[16,128]{1,0:T(8,128)S(1)} %add.10), channel_id=1, source_target_pairs={{0,28},{4,24},{8,20},{12,16},{16,12},{20,8},{24,4},{28,0},{1,29},{... | collective-permute-start | bytes 24584 | tf_op jit(solution)/shard_map/ppermute | solution.py:199
  100.7 2.8 %convolution_bitcast_fusion = f32[1,1024,1024]{2,1,0:T(8,128)} fusion(bf16[256,1024]{1,0:T(8,128)(2,1)S(1)} %get-tuple-element.5, bf16[256,1024]{1,0:T(8,128)(2,1)S(1)} %get-tuple-element.6), kind=kOutput, calls=%fused_computation | convolution fusion | flops 536870912 | bytes 5242880 | tf_op jit(solution)/shard_map/dot_general | solution.py:200
  103.5 2.4 %collective-permute-done.2 = f32[16,128]{1,0:T(8,128)S(1)} collective-permute-done((f32[16,128]{1,0:T(8,128)S(1)}, f32[16,128]{1,0:T(8,128)S(1)}, u32[]{:S(2)}, u32[]{:S(2)}) %collective-permute-start.2) | collective-permute-done | bytes 8224 | tf_op jit(solution)/shard_map/ppermute | solution.py:199
  105.9 0.6 divide_bitcast_fusion
  (3 shorter events, 0.0 us)
Async XLA Ops:
  0.6 66.7 %copy-start = (f32[1,1024,64]{1,2,0:T(8,128)S(1)}, f32[1,1024,64]{1,2,0:T(8,128)}, u32[]{:S(2)}) copy-start(f32[1,1024,64]{1,2,0:T(8,128)} %param.5) | copy-start | bytes 786436
  91.0 3.7 %collective-permute-start = (f32[16,128]{1,0:T(8,128)S(1)}, f32[16,128]{1,0:T(8,128)S(1)}, u32[]{:S(2)}, u32[]{:S(2)}) collective-permute-start(f32[16,128]{1,0:T(8,128)S(1)} %reduce_sum.9), channel_id=1, source_target_pairs={{0,4},{4,0},{1,5},{5,1},{2,6},{6,2},{3,7},{7,3},{8,12},{12,8},{9,1... | collective-permute-start | bytes 24584 | tf_op jit(solution)/shard_map/ppermute | solution.py:198
  94.7 4.5 %collective-permute-start.1 = (f32[16,128]{1,0:T(8,128)S(1)}, f32[16,128]{1,0:T(8,128)S(1)}, u32[]{:S(2)}, u32[]{:S(2)}) collective-permute-start(f32[16,128]{1,0:T(8,128)S(1)} %add.9), channel_id=1, source_target_pairs={{0,8},{8,0},{1,9},{9,1},{2,10},{10,2},{3,11},{11,3},{4,12},{12,4},... | collective-permute-start | bytes 24584 | tf_op jit(solution)/shard_map/ppermute | solution.py:198
  99.2 6.7 %collective-permute-start.2 = (f32[16,128]{1,0:T(8,128)S(1)}, f32[16,128]{1,0:T(8,128)S(1)}, u32[]{:S(2)}, u32[]{:S(2)}) collective-permute-start(f32[16,128]{1,0:T(8,128)S(1)} %add.10), channel_id=1, source_target_pairs={{0,28},{4,24},{8,20},{12,16},{16,12},{20,8},{24,4},{28,0},{1,29},{... | collective-permute-start | bytes 24584 | tf_op jit(solution)/shard_map/ppermute | solution.py:199

commit v4 on v3

--- a/solution.py
+++ b/solution.py
@@ -15,6 +15,7 @@
 ITERS = 3
 PARTS = 3
 CHUNKS = 4
+WIDTHS = (8, 8, 16, 16, 16)
 AXES = ("x", "yl", "z2", "z1", "z0", "yh", "c")
 PLANE = ("x", "yl", "yh", "c")
 PLANE_SIZE = 32
@@ -80,29 +81,35 @@
         wide = jnp.concatenate([gram[8 * q : 8 * q + 8], jnp.zeros((8, N), jnp.float32)], axis=1)
         a.append(wide + eye)
     done = []
-    for k in range(blocks):
-        below = range(k, blocks)
-        cols = [[lanes(a[q], 8 * k + i) for q in below] for i in range(8)]
+    first = 0
+    for width in WIDTHS:
+        top = first // 8
+        near = width // 8
+        cols = [[lanes(a[q], first + i) if q >= top + i // 8 else None for q in range(top, blocks)] for i in range(width)]
         scaled = []
-        for i in range(8):
-            r = lax.rsqrt(rows(cols[i][0], i))
-            l = [c * r for c in cols[i]]
-            cols[i] = l
-            for i2 in range(i + 1, 8):
-                t = rows(l[0], i2)
-                cols[i2] = [c - m * t for c, m in zip(cols[i2], l)]
-            this = rows(a[k], i)
+        for i in range(width):
+            g = i // 8
+            r = lax.rsqrt(rows(cols[i][g], i % 8))
+            cols[i] = [None if c is None else c * r for c in cols[i]]
+            l = cols[i]
+            for i2 in range(i + 1, width):
+                t = rows(l[i2 // 8], i2 % 8)
+                cols[i2] = [None if c is None else c - m * t for c, m in zip(cols[i2], l)]
+            this = rows(a[top + g], i % 8)
             for i1 in range(i):
-                this = this - rows(cols[i1][0], i) * scaled[i1]
+                this = this - rows(cols[i1][g], i % 8) * scaled[i1]
             scaled.append(this * r)
-        out = scaled[0]
-        for i in range(1, 8):
-            out = jnp.where(row == i, scaled[i], out)
-        done.append(out)
-        for q in range(k + 1, blocks):
-            for i in range(8):
-                a[q] = a[q] - cols[i][q - k] * scaled[i]
-        beside(k)
+        for g in range(near):
+            out = scaled[8 * g]
+            for i in range(1, 8):
+                out = jnp.where(row == i, scaled[8 * g + i], out)
+            done.append(out)
+        for q in range(top + near, blocks):
+            for i in range(width):
+                a[q] = a[q] - cols[i][q - top] * scaled[i]
+        for g in range(near):
+            beside(top + g)
+        first += width
     return jnp.concatenate(done, axis=0)[:, N:]
 
 
@@ -194,8 +201,11 @@
     owned = lax.all_to_all(data, AXES, split_axis=0, concat_axis=0, tiled=True)
     noise, left, right = subspace(owned, steering[0], start[0].T)
     total = lax.all_to_all(noise, PLANE, split_axis=0, concat_axis=0, tiled=True).sum(0)
-    for axis in ("z0", "z1"):
-        total = total + lax.ppermute(total, axis, [(0, 1), (1, 0)])
+    swap = [(0, 1), (1, 0)]
+    one = lax.ppermute(total, "z0", swap)
+    two = lax.ppermute(total, "z1", swap)
+    three = lax.ppermute(total, ("z1", "z0"), [(z, 3 - z) for z in range(4)])
+    total = (total + one) + (two + three)
     total = total + lax.ppermute(total, ("z2", "z1", "z0"), [(z, 7 - z) for z in range(8)])
     projector = lax.dot_general(
         left, right, (((0,), (0,)), ((), ())), preferred_element_type=jnp.float32

time: 107 us -> 105 us (0.981)
  waiting for transfers between devices: 9.2 us -> 5.91 us
  starting transfers between devices: 2.99 us -> 5.12 us
    ppermute x2 -> x3, waiting for transfers between devices: 6.76 us -> 3.55 us  [the longest x1 1.88 us: on_device(): one = lax.ppermute(total, 'z0', swap)]
    ppermute x2 -> x3, starting transfers between devices: 1.52 us -> 3.57 us  [the longest x1 2.86 us: on_device(): two = lax.ppermute(total, 'z1', swap)]
  transfers between devices with their start and end apart: 3 -> 4, of which waited for: 3 -> 4; matrix products, arithmetic and copies ran while one was open for 3% -> 3% of each run, Pallas kernels for 0% -> 0%
where the time goes in v4:
time: 105 us
  blocking collectives  80.7 us (77%)
  Pallas kernels  8.94 us (9%)
  waiting for transfers between devices  5.91 us (6%)
  starting transfers between devices  5.12 us (5%)
  matrix products  2.76 us (3%)
    all_to_all x1, blocking collectives, on_device(): owned = lax.all_to_all(data, AXES, split_axis=0, concat_axis=0, tiled=True)  66.7 us
    all_to_all x1, blocking collectives, on_device(): lax.all_to_all(noise, PLANE, split_axis=0, concat_axis=0, tiled=True).sum(0)  13.9 us
    pallas_call x1, Pallas kernels, subspace(): pl.pallas_call(subspace_kernel, out_shape=(jax.ShapeDtypeStruct((PLANE_SI...  8.94 us
    ppermute x1, starting transfers between devices, on_device(): two = lax.ppermute(total, 'z1', swap)  2.86 us
    dot_general x1, matrix products, on_device(): lax.dot_general(left, right, (((0,), (0,)), ((), ())), preferred_element_...  2.76 us
    ppermute x1, waiting for transfers between devices, on_device(): lax.ppermute(total, ('z2', 'z1', 'z0'), [(z, 7 - z) for z in range(8)])  2.36 us
  transfers between devices with their start and end apart: 4, of which 4 were waited for; matrix products, arithmetic and copies ran while one was open for 3% of the time, Pallas kernels for 0%

profile of v4, /device:TPU:32, one launch (start us, length us, event | category | flops | bytes accessed | tf_op | source)
XLA Modules:
  0.0 104.7 jit_solution(12376617933621572040)
XLA Ops:
  0.6 0.0 copy-start
  0.6 66.7 %all_to_all.10.data_ref = bf16[256,4,1024]{2,1,0:T(4,128)(2,1)S(1)} all-to-all(bf16[256,4,1024]{2,1,0:T(4,128)(2,1)} %param.3), channel_id=1, replica_groups=mesh['x'=4,'yl'=2,'z2'=2,'z1'=2,'z0'=2,'yh'=2,'c'=2] {'x','yl','z2','z1'..., dimensions={0} | all-to-all | bytes 4194304 | tf_op jit(solution)/shard_map/all_to_all | solution.py:201
  67.4 0.0 copy-done
  67.4 8.9 %subspace.1 = (f32[32,16,128]{2,1,0:T(8,128)S(1)}, bf16[256,1024]{1,0:T(8,128)(2,1)S(1)}, bf16[256,1024]{1,0:T(8,128)(2,1)S(1)}) custom-call(bf16[256,4,1024]{2,1,0:T(4,128)(2,1)S(1)} %all_to_all.10.data_ref, bf16[1024,2048]{1,0:T(8,128)(2,1)} %bitcast.11, f32[64,1024]{1,0:T(8,128)S(1)} %bitcast.10), custom_call_target="tpu_custom_call" | custom-call | tf_op jit(solution)/shard_map/subspace/pallas_call | solution.py:178
  76.3 13.9 %all_to_all.11 = f32[32,16,128]{2,1,0:T(8,128)S(1)} all-to-all(f32[32,16,128]{2,1,0:T(8,128)S(1)} %get-tuple-element.7), channel_id=1, replica_groups=mesh['x'=4,'yl'=2,'z2'=2,'z1'=2,'z0'=2,'yh'=2,'c'=2] {'x','yl','yh','c'}, dimensions={0} | all-to-all | bytes 524288 | tf_op jit(solution)/shard_map/all_to_all | solution.py:203
  90.3 0.6 collective-permute-start.2
  90.9 2.9 %collective-permute-start.1 = (f32[16,128]{1,0:T(8,128)S(1)}, f32[16,128]{1,0:T(8,128)S(1)}, u32[]{:S(2)}, u32[]{:S(2)}) collective-permute-start(f32[16,128]{1,0:T(8,128)S(1)} %reduce_sum.9), channel_id=1, source_target_pairs={{0,8},{8,0},{1,9},{9,1},{2,10},{10,2},{3,11},{11,3},{4,12},{12,4},... | collective-permute-start | bytes 24584 | tf_op jit(solution)/shard_map/ppermute | solution.py:206
  93.8 0.1 collective-permute-start
  93.9 0.2 collective-permute-done.2
  94.0 1.5 %collective-permute-done.1 = f32[16,128]{1,0:T(8,128)S(1)} collective-permute-done((f32[16,128]{1,0:T(8,128)S(1)}, f32[16,128]{1,0:T(8,128)S(1)}, u32[]{:S(2)}, u32[]{:S(2)}) %collective-permute-start.1) | collective-permute-done | bytes 8224 | tf_op jit(solution)/shard_map/ppermute | solution.py:206
  95.6 1.9 %collective-permute-done = f32[16,128]{1,0:T(8,128)S(1)} collective-permute-done((f32[16,128]{1,0:T(8,128)S(1)}, f32[16,128]{1,0:T(8,128)S(1)}, u32[]{:S(2)}, u32[]{:S(2)}) %collective-permute-start) | collective-permute-done | bytes 8224 | tf_op jit(solution)/shard_map/ppermute | solution.py:205
  97.4 1.5 %collective-permute-start.3 = (f32[16,128]{1,0:T(8,128)S(1)}, f32[16,128]{1,0:T(8,128)S(1)}, u32[]{:S(2)}, u32[]{:S(2)}) collective-permute-start(f32[16,128]{1,0:T(8,128)S(1)} %add_add_fusion), channel_id=1, source_target_pairs={{0,28},{4,24},{8,20},{12,16},{16,12},{20,8},{24,4},{28,0},{1,29},{... | collective-permute-start | bytes 24584 | tf_op jit(solution)/shard_map/ppermute | solution.py:209
  99.0 2.8 %convolution_bitcast_fusion = f32[1,1024,1024]{2,1,0:T(8,128)} fusion(bf16[256,1024]{1,0:T(8,128)(2,1)S(1)} %get-tuple-element.5, bf16[256,1024]{1,0:T(8,128)(2,1)S(1)} %get-tuple-element.6), kind=kOutput, calls=%fused_computation | convolution fusion | flops 536870912 | bytes 5242880 | tf_op jit(solution)/shard_map/dot_general | solution.py:210
  101.7 2.4 %collective-permute-done.3 = f32[16,128]{1,0:T(8,128)S(1)} collective-permute-done((f32[16,128]{1,0:T(8,128)S(1)}, f32[16,128]{1,0:T(8,128)S(1)}, u32[]{:S(2)}, u32[]{:S(2)}) %collective-permute-start.3) | collective-permute-done | bytes 8224 | tf_op jit(solution)/shard_map/ppermute | solution.py:209
  104.1 0.6 divide_bitcast_fusion
  (2 shorter events, 0.0 us)
Async XLA Ops:
  0.6 66.7 %copy-start = (f32[1,1024,64]{1,2,0:T(8,128)S(1)}, f32[1,1024,64]{1,2,0:T(8,128)}, u32[]{:S(2)}) copy-start(f32[1,1024,64]{1,2,0:T(8,128)} %param.5) | copy-start | bytes 786436
  90.3 3.7 %collective-permute-start.2 = (f32[16,128]{1,0:T(8,128)S(1)}, f32[16,128]{1,0:T(8,128)S(1)}, u32[]{:S(2)}, u32[]{:S(2)}) collective-permute-start(f32[16,128]{1,0:T(8,128)S(1)} %reduce_sum.9), channel_id=1, source_target_pairs={{0,12},{4,8},{8,4},{12,0},{1,13},{5,9},{9,5},{13,1},{2,14},{6,10},... | collective-permute-start | bytes 24584 | tf_op jit(solution)/shard_map/ppermute | solution.py:207
  90.9 4.6 %collective-permute-start.1 = (f32[16,128]{1,0:T(8,128)S(1)}, f32[16,128]{1,0:T(8,128)S(1)}, u32[]{:S(2)}, u32[]{:S(2)}) collective-permute-start(f32[16,128]{1,0:T(8,128)S(1)} %reduce_sum.9), channel_id=1, source_target_pairs={{0,8},{8,0},{1,9},{9,1},{2,10},{10,2},{3,11},{11,3},{4,12},{12,4},... | collective-permute-start | bytes 24584 | tf_op jit(solution)/shard_map/ppermute | solution.py:206
  93.8 3.7 %collective-permute-start = (f32[16,128]{1,0:T(8,128)S(1)}, f32[16,128]{1,0:T(8,128)S(1)}, u32[]{:S(2)}, u32[]{:S(2)}) collective-permute-start(f32[16,128]{1,0:T(8,128)S(1)} %reduce_sum.9), channel_id=1, source_target_pairs={{0,4},{4,0},{1,5},{5,1},{2,6},{6,2},{3,7},{7,3},{8,12},{12,8},{9,1... | collective-permute-start | bytes 24584 | tf_op jit(solution)/shard_map/ppermute | solution.py:205
  97.4 6.7 %collective-permute-start.3 = (f32[16,128]{1,0:T(8,128)S(1)}, f32[16,128]{1,0:T(8,128)S(1)}, u32[]{:S(2)}, u32[]{:S(2)}) collective-permute-start(f32[16,128]{1,0:T(8,128)S(1)} %add_add_fusion), channel_id=1, source_target_pairs={{0,28},{4,24},{8,20},{12,16},{16,12},{20,8},{24,4},{28,0},{1,29},{... | collective-permute-start | bytes 24584 | tf_op jit(solution)/shard_map/ppermute | solution.py:209

commit v5 on v4

--- a/solution.py
+++ b/solution.py
@@ -87,18 +87,28 @@
         near = width // 8
         cols = [[lanes(a[q], first + i) if q >= top + i // 8 else None for q in range(top, blocks)] for i in range(width)]
         scaled = []
-        for i in range(width):
+        factor = [[] for _ in range(width)]
+        for i in range(0, width, 2):
             g = i // 8
-            r = lax.rsqrt(rows(cols[i][g], i % 8))
-            cols[i] = [None if c is None else c * r for c in cols[i]]
-            l = cols[i]
-            for i2 in range(i + 1, width):
-                t = rows(l[i2 // 8], i2 % 8)
-                cols[i2] = [None if c is None else c - m * t for c, m in zip(cols[i2], l)]
-            this = rows(a[top + g], i % 8)
-            for i1 in range(i):
-                this = this - rows(cols[i1][g], i % 8) * scaled[i1]
-            scaled.append(this * r)
+            one = rows(cols[i][g], i % 8)
+            cross = rows(cols[i][g], i % 8 + 1)
+            two = rows(cols[i + 1][g], i % 8 + 1)
+            r1 = lax.rsqrt(one)
+            t = cross * r1
+            r2 = lax.rsqrt(two - t * t)
+            cols[i] = [None if c is None else c * r1 for c in cols[i]]
+            cols[i + 1] = [None if c is None else (c - m * t) * r2 for c, m in zip(cols[i + 1], cols[i])]
+            factor[i + 1].append(t)
+            for i2 in range(i + 2, width):
+                t1 = rows(cols[i][i2 // 8], i2 % 8)
+                t2 = rows(cols[i + 1][i2 // 8], i2 % 8)
+                factor[i2] += [t1, t2]
+                cols[i2] = [None if c is None else c - (m1 * t1 + m2 * t2) for c, m1, m2 in zip(cols[i2], cols[i], cols[i + 1])]
+            for s, r in ((i, r1), (i + 1, r2)):
+                this = rows(a[top + g], s % 8)
+                for t, line in zip(factor[s], scaled):
+                    this = this - t * line
+                scaled.append(this * r)
         for g in range(near):
             out = scaled[8 * g]
             for i in range(1, 8):

time: 105 us -> 105 us (level)
  no operation moved by 1% of the time
where the time goes in v5:
time: 105 us
  blocking collectives  80.7 us (77%)
  Pallas kernels  8.78 us (8%)
  waiting for transfers between devices  5.9 us (6%)
  starting transfers between devices  5.12 us (5%)
  matrix products  2.76 us (3%)
    all_to_all x1, blocking collectives, on_device(): owned = lax.all_to_all(data, AXES, split_axis=0, concat_axis=0, tiled=True)  66.7 us
    all_to_all x1, blocking collectives, on_device(): lax.all_to_all(noise, PLANE, split_axis=0, concat_axis=0, tiled=True).sum(0)  14 us
    pallas_call x1, Pallas kernels, subspace(): pl.pallas_call(subspace_kernel, out_shape=(jax.ShapeDtypeStruct((PLANE_SI...  8.78 us
    ppermute x1, starting transfers between devices, on_device(): two = lax.ppermute(total, 'z1', swap)  2.85 us
    dot_general x1, matrix products, on_device(): lax.dot_general(left, right, (((0,), (0,)), ((), ())), preferred_element_...  2.76 us
    ppermute x1, waiting for transfers between devices, on_device(): lax.ppermute(total, ('z2', 'z1', 'z0'), [(z, 7 - z) for z in range(8)])  2.36 us
  transfers between devices with their start and end apart: 4, of which 4 were waited for; matrix products, arithmetic and copies ran while one was open for 3% of the time, Pallas kernels for 0%

profile of v5, /device:TPU:32, one launch (start us, length us, event | category | flops | bytes accessed | tf_op | source)
XLA Modules:
  0.0 104.6 jit_solution(7974492882287382945)
XLA Ops:
  0.6 0.0 copy-start
  0.6 66.7 %all_to_all.10.data_ref = bf16[256,4,1024]{2,1,0:T(4,128)(2,1)S(1)} all-to-all(bf16[256,4,1024]{2,1,0:T(4,128)(2,1)} %param.3), channel_id=1, replica_groups=mesh['x'=4,'yl'=2,'z2'=2,'z1'=2,'z0'=2,'yh'=2,'c'=2] {'x','yl','z2','z1'..., dimensions={0} | all-to-all | bytes 4194304 | tf_op jit(solution)/shard_map/all_to_all | solution.py:211
  67.4 0.0 copy-done
  67.4 8.8 %subspace.1 = (f32[32,16,128]{2,1,0:T(8,128)S(1)}, bf16[256,1024]{1,0:T(8,128)(2,1)S(1)}, bf16[256,1024]{1,0:T(8,128)(2,1)S(1)}) custom-call(bf16[256,4,1024]{2,1,0:T(4,128)(2,1)S(1)} %all_to_all.10.data_ref, bf16[1024,2048]{1,0:T(8,128)(2,1)} %bitcast.11, f32[64,1024]{1,0:T(8,128)S(1)} %bitcast.10), custom_call_target="tpu_custom_call" | custom-call | tf_op jit(solution)/shard_map/subspace/pallas_call | solution.py:188
  76.2 14.0 %all_to_all.11 = f32[32,16,128]{2,1,0:T(8,128)S(1)} all-to-all(f32[32,16,128]{2,1,0:T(8,128)S(1)} %get-tuple-element.7), channel_id=1, replica_groups=mesh['x'=4,'yl'=2,'z2'=2,'z1'=2,'z0'=2,'yh'=2,'c'=2] {'x','yl','yh','c'}, dimensions={0} | all-to-all | bytes 524288 | tf_op jit(solution)/shard_map/all_to_all | solution.py:213
  90.2 0.6 collective-permute-start.2
  90.8 2.9 %collective-permute-start.1 = (f32[16,128]{1,0:T(8,128)S(1)}, f32[16,128]{1,0:T(8,128)S(1)}, u32[]{:S(2)}, u32[]{:S(2)}) collective-permute-start(f32[16,128]{1,0:T(8,128)S(1)} %reduce_sum.9), channel_id=1, source_target_pairs={{0,8},{8,0},{1,9},{9,1},{2,10},{10,2},{3,11},{11,3},{4,12},{12,4},... | collective-permute-start | bytes 24584 | tf_op jit(solution)/shard_map/ppermute | solution.py:216
  93.6 0.1 collective-permute-start
  93.7 0.2 collective-permute-done.2
  93.9 1.5 %collective-permute-done.1 = f32[16,128]{1,0:T(8,128)S(1)} collective-permute-done((f32[16,128]{1,0:T(8,128)S(1)}, f32[16,128]{1,0:T(8,128)S(1)}, u32[]{:S(2)}, u32[]{:S(2)}) %collective-permute-start.1) | collective-permute-done | bytes 8224 | tf_op jit(solution)/shard_map/ppermute | solution.py:216
  95.4 1.9 %collective-permute-done = f32[16,128]{1,0:T(8,128)S(1)} collective-permute-done((f32[16,128]{1,0:T(8,128)S(1)}, f32[16,128]{1,0:T(8,128)S(1)}, u32[]{:S(2)}, u32[]{:S(2)}) %collective-permute-start) | collective-permute-done | bytes 8224 | tf_op jit(solution)/shard_map/ppermute | solution.py:215
  97.3 1.5 %collective-permute-start.3 = (f32[16,128]{1,0:T(8,128)S(1)}, f32[16,128]{1,0:T(8,128)S(1)}, u32[]{:S(2)}, u32[]{:S(2)}) collective-permute-start(f32[16,128]{1,0:T(8,128)S(1)} %add_add_fusion), channel_id=1, source_target_pairs={{0,28},{4,24},{8,20},{12,16},{16,12},{20,8},{24,4},{28,0},{1,29},{... | collective-permute-start | bytes 24584 | tf_op jit(solution)/shard_map/ppermute | solution.py:219
  98.8 2.8 %convolution_bitcast_fusion = f32[1,1024,1024]{2,1,0:T(8,128)} fusion(bf16[256,1024]{1,0:T(8,128)(2,1)S(1)} %get-tuple-element.5, bf16[256,1024]{1,0:T(8,128)(2,1)S(1)} %get-tuple-element.6), kind=kOutput, calls=%fused_computation | convolution fusion | flops 536870912 | bytes 5242880 | tf_op jit(solution)/shard_map/dot_general | solution.py:220
  101.6 2.4 %collective-permute-done.3 = f32[16,128]{1,0:T(8,128)S(1)} collective-permute-done((f32[16,128]{1,0:T(8,128)S(1)}, f32[16,128]{1,0:T(8,128)S(1)}, u32[]{:S(2)}, u32[]{:S(2)}) %collective-permute-start.3) | collective-permute-done | bytes 8224 | tf_op jit(solution)/shard_map/ppermute | solution.py:219
  103.9 0.6 divide_bitcast_fusion
  (2 shorter events, 0.0 us)
Async XLA Ops:
  0.6 66.7 %copy-start = (f32[1,1024,64]{1,2,0:T(8,128)S(1)}, f32[1,1024,64]{1,2,0:T(8,128)}, u32[]{:S(2)}) copy-start(f32[1,1024,64]{1,2,0:T(8,128)} %param.5) | copy-start | bytes 786436
  90.2 3.7 %collective-permute-start.2 = (f32[16,128]{1,0:T(8,128)S(1)}, f32[16,128]{1,0:T(8,128)S(1)}, u32[]{:S(2)}, u32[]{:S(2)}) collective-permute-start(f32[16,128]{1,0:T(8,128)S(1)} %reduce_sum.9), channel_id=1, source_target_pairs={{0,12},{4,8},{8,4},{12,0},{1,13},{5,9},{9,5},{13,1},{2,14},{6,10},... | collective-permute-start | bytes 24584 | tf_op jit(solution)/shard_map/ppermute | solution.py:217
  90.8 4.6 %collective-permute-start.1 = (f32[16,128]{1,0:T(8,128)S(1)}, f32[16,128]{1,0:T(8,128)S(1)}, u32[]{:S(2)}, u32[]{:S(2)}) collective-permute-start(f32[16,128]{1,0:T(8,128)S(1)} %reduce_sum.9), channel_id=1, source_target_pairs={{0,8},{8,0},{1,9},{9,1},{2,10},{10,2},{3,11},{11,3},{4,12},{12,4},... | collective-permute-start | bytes 24584 | tf_op jit(solution)/shard_map/ppermute | solution.py:216
  93.6 3.7 %collective-permute-start = (f32[16,128]{1,0:T(8,128)S(1)}, f32[16,128]{1,0:T(8,128)S(1)}, u32[]{:S(2)}, u32[]{:S(2)}) collective-permute-start(f32[16,128]{1,0:T(8,128)S(1)} %reduce_sum.9), channel_id=1, source_target_pairs={{0,4},{4,0},{1,5},{5,1},{2,6},{6,2},{3,7},{7,3},{8,12},{12,8},{9,1... | collective-permute-start | bytes 24584 | tf_op jit(solution)/shard_map/ppermute | solution.py:215
  97.3 6.7 %collective-permute-start.3 = (f32[16,128]{1,0:T(8,128)S(1)}, f32[16,128]{1,0:T(8,128)S(1)}, u32[]{:S(2)}, u32[]{:S(2)}) collective-permute-start(f32[16,128]{1,0:T(8,128)S(1)} %add_add_fusion), channel_id=1, source_target_pairs={{0,28},{4,24},{8,20},{12,16},{16,12},{20,8},{24,4},{28,0},{1,29},{... | collective-permute-start | bytes 24584 | tf_op jit(solution)/shard_map/ppermute | solution.py:219

commit v6 on v5

--- a/solution.py
+++ b/solution.py
@@ -15,7 +15,7 @@
 ITERS = 3
 PARTS = 3
 CHUNKS = 4
-WIDTHS = (8, 8, 16, 16, 16)
+WIDTHS = (16, 16, 16, 16)
 AXES = ("x", "yl", "z2", "z1", "z0", "yh", "c")
 PLANE = ("x", "yl", "yh", "c")
 PLANE_SIZE = 32

time: 105 us -> 105 us (level)
  no operation moved by 1% of the time
where the time goes in v6:
time: 105 us; the launch traced here: 104 us
  blocking collectives  80.7 us (77%)
  Pallas kernels  8.68 us (8%)
  waiting for transfers between devices  5.91 us (6%)
  starting transfers between devices  5.12 us (5%)
  matrix products  2.76 us (3%)
    all_to_all x1, blocking collectives, on_device(): owned = lax.all_to_all(data, AXES, split_axis=0, concat_axis=0, tiled=True)  66.7 us
    all_to_all x1, blocking collectives, on_device(): lax.all_to_all(noise, PLANE, split_axis=0, concat_axis=0, tiled=True).sum(0)  13.9 us
    pallas_call x1, Pallas kernels, subspace(): pl.pallas_call(subspace_kernel, out_shape=(jax.ShapeDtypeStruct((PLANE_SI...  8.68 us
    ppermute x1, starting transfers between devices, on_device(): two = lax.ppermute(total, 'z1', swap)  2.86 us
    dot_general x1, matrix products, on_device(): lax.dot_general(left, right, (((0,), (0,)), ((), ())), preferred_element_...  2.76 us
    ppermute x1, waiting for transfers between devices, on_device(): lax.ppermute(total, ('z2', 'z1', 'z0'), [(z, 7 - z) for z in range(8)])  2.36 us
  transfers between devices with their start and end apart: 4, of which 4 were waited for; matrix products, arithmetic and copies ran while one was open for 3% of the time, Pallas kernels for 0%

profile of v6, /device:TPU:32, one launch (start us, length us, event | category | flops | bytes accessed | tf_op | source)
XLA Modules:
  0.0 104.5 jit_solution(8216756184035902517)
XLA Ops:
  0.6 0.0 copy-start
  0.6 66.7 %all_to_all.10.data_ref = bf16[256,4,1024]{2,1,0:T(4,128)(2,1)S(1)} all-to-all(bf16[256,4,1024]{2,1,0:T(4,128)(2,1)} %param.3), channel_id=1, replica_groups=mesh['x'=4,'yl'=2,'z2'=2,'z1'=2,'z0'=2,'yh'=2,'c'=2] {'x','yl','z2','z1'..., dimensions={0} | all-to-all | bytes 4194304 | tf_op jit(solution)/shard_map/all_to_all | solution.py:211
  67.4 0.0 copy-done
  67.4 8.7 %subspace.1 = (f32[32,16,128]{2,1,0:T(8,128)S(1)}, bf16[256,1024]{1,0:T(8,128)(2,1)S(1)}, bf16[256,1024]{1,0:T(8,128)(2,1)S(1)}) custom-call(bf16[256,4,1024]{2,1,0:T(4,128)(2,1)S(1)} %all_to_all.10.data_ref, bf16[1024,2048]{1,0:T(8,128)(2,1)} %bitcast.11, f32[64,1024]{1,0:T(8,128)S(1)} %bitcast.10), custom_call_target="tpu_custom_call" | custom-call | tf_op jit(solution)/shard_map/subspace/pallas_call | solution.py:188
  76.1 13.9 %all_to_all.11 = f32[32,16,128]{2,1,0:T(8,128)S(1)} all-to-all(f32[32,16,128]{2,1,0:T(8,128)S(1)} %get-tuple-element.7), channel_id=1, replica_groups=mesh['x'=4,'yl'=2,'z2'=2,'z1'=2,'z0'=2,'yh'=2,'c'=2] {'x','yl','yh','c'}, dimensions={0} | all-to-all | bytes 524288 | tf_op jit(solution)/shard_map/all_to_all | solution.py:213
  90.0 0.6 collective-permute-start.2
  90.7 2.9 %collective-permute-start.1 = (f32[16,128]{1,0:T(8,128)S(1)}, f32[16,128]{1,0:T(8,128)S(1)}, u32[]{:S(2)}, u32[]{:S(2)}) collective-permute-start(f32[16,128]{1,0:T(8,128)S(1)} %reduce_sum.9), channel_id=1, source_target_pairs={{0,8},{8,0},{1,9},{9,1},{2,10},{10,2},{3,11},{11,3},{4,12},{12,4},... | collective-permute-start | bytes 24584 | tf_op jit(solution)/shard_map/ppermute | solution.py:216
  93.5 0.1 collective-permute-start
  93.6 0.2 collective-permute-done.2
  93.8 1.5 %collective-permute-done.1 = f32[16,128]{1,0:T(8,128)S(1)} collective-permute-done((f32[16,128]{1,0:T(8,128)S(1)}, f32[16,128]{1,0:T(8,128)S(1)}, u32[]{:S(2)}, u32[]{:S(2)}) %collective-permute-start.1) | collective-permute-done | bytes 8224 | tf_op jit(solution)/shard_map/ppermute | solution.py:216
  95.3 1.9 %collective-permute-done = f32[16,128]{1,0:T(8,128)S(1)} collective-permute-done((f32[16,128]{1,0:T(8,128)S(1)}, f32[16,128]{1,0:T(8,128)S(1)}, u32[]{:S(2)}, u32[]{:S(2)}) %collective-permute-start) | collective-permute-done | bytes 8224 | tf_op jit(solution)/shard_map/ppermute | solution.py:215
  97.2 1.5 %collective-permute-start.3 = (f32[16,128]{1,0:T(8,128)S(1)}, f32[16,128]{1,0:T(8,128)S(1)}, u32[]{:S(2)}, u32[]{:S(2)}) collective-permute-start(f32[16,128]{1,0:T(8,128)S(1)} %add_add_fusion), channel_id=1, source_target_pairs={{0,28},{4,24},{8,20},{12,16},{16,12},{20,8},{24,4},{28,0},{1,29},{... | collective-permute-start | bytes 24584 | tf_op jit(solution)/shard_map/ppermute | solution.py:219
  98.7 2.8 %convolution_bitcast_fusion = f32[1,1024,1024]{2,1,0:T(8,128)} fusion(bf16[256,1024]{1,0:T(8,128)(2,1)S(1)} %get-tuple-element.5, bf16[256,1024]{1,0:T(8,128)(2,1)S(1)} %get-tuple-element.6), kind=kOutput, calls=%fused_computation | convolution fusion | flops 536870912 | bytes 5242880 | tf_op jit(solution)/shard_map/dot_general | solution.py:220
  101.5 2.4 %collective-permute-done.3 = f32[16,128]{1,0:T(8,128)S(1)} collective-permute-done((f32[16,128]{1,0:T(8,128)S(1)}, f32[16,128]{1,0:T(8,128)S(1)}, u32[]{:S(2)}, u32[]{:S(2)}) %collective-permute-start.3) | collective-permute-done | bytes 8224 | tf_op jit(solution)/shard_map/ppermute | solution.py:219
  103.8 0.6 divide_bitcast_fusion
  (2 shorter events, 0.0 us)
Async XLA Ops:
  0.6 66.7 %copy-start = (f32[1,1024,64]{1,2,0:T(8,128)S(1)}, f32[1,1024,64]{1,2,0:T(8,128)}, u32[]{:S(2)}) copy-start(f32[1,1024,64]{1,2,0:T(8,128)} %param.5) | copy-start | bytes 786436
  90.0 3.7 %collective-permute-start.2 = (f32[16,128]{1,0:T(8,128)S(1)}, f32[16,128]{1,0:T(8,128)S(1)}, u32[]{:S(2)}, u32[]{:S(2)}) collective-permute-start(f32[16,128]{1,0:T(8,128)S(1)} %reduce_sum.9), channel_id=1, source_target_pairs={{0,12},{4,8},{8,4},{12,0},{1,13},{5,9},{9,5},{13,1},{2,14},{6,10},... | collective-permute-start | bytes 24584 | tf_op jit(solution)/shard_map/ppermute | solution.py:217
  90.7 4.6 %collective-permute-start.1 = (f32[16,128]{1,0:T(8,128)S(1)}, f32[16,128]{1,0:T(8,128)S(1)}, u32[]{:S(2)}, u32[]{:S(2)}) collective-permute-start(f32[16,128]{1,0:T(8,128)S(1)} %reduce_sum.9), channel_id=1, source_target_pairs={{0,8},{8,0},{1,9},{9,1},{2,10},{10,2},{3,11},{11,3},{4,12},{12,4},... | collective-permute-start | bytes 24584 | tf_op jit(solution)/shard_map/ppermute | solution.py:216
  93.5 3.7 %collective-permute-start = (f32[16,128]{1,0:T(8,128)S(1)}, f32[16,128]{1,0:T(8,128)S(1)}, u32[]{:S(2)}, u32[]{:S(2)}) collective-permute-start(f32[16,128]{1,0:T(8,128)S(1)} %reduce_sum.9), channel_id=1, source_target_pairs={{0,4},{4,0},{1,5},{5,1},{2,6},{6,2},{3,7},{7,3},{8,12},{12,8},{9,1... | collective-permute-start | bytes 24584 | tf_op jit(solution)/shard_map/ppermute | solution.py:215
  97.2 6.7 %collective-permute-start.3 = (f32[16,128]{1,0:T(8,128)S(1)}, f32[16,128]{1,0:T(8,128)S(1)}, u32[]{:S(2)}, u32[]{:S(2)}) collective-permute-start(f32[16,128]{1,0:T(8,128)S(1)} %add_add_fusion), channel_id=1, source_target_pairs={{0,28},{4,24},{8,20},{12,16},{16,12},{20,8},{24,4},{28,0},{1,29},{... | collective-permute-start | bytes 24584 | tf_op jit(solution)/shard_map/ppermute | solution.py:219
